TPU v7x, 32 devices: a whole 2x2x4 slice. The times are simulated.
32 devices in a mesh: dp: 2 (over x), context: 16 (over z, y, core).
Axes of the slice: x: 2, y: 2, z: 4, core: 2. Of those that a mesh axis runs over, the one named last changes fastest.
Arguments:
- queries: bfloat16 [2, 2048, 2048], P('dp', 'context'), may hold values from -6 to 6
- key_rows: bfloat16 [2, 2048, 2048], P('dp', 'context'), may hold values from -6 to 6
- value_rows: bfloat16 [2, 2048, 2048], P('dp', 'context'), may hold values from -6 to 6
- out_grad: bfloat16 [2, 2048, 2048], P('dp', 'context'), may hold values from -6 to 6
- feature_maps: bfloat16 [16, 128, 128], replicated, may hold values from -0.5 to 0.5
Outputs:
- query_grad: bfloat16 [2, 2048, 2048], P('dp', 'context')
- key_grad: bfloat16 [2, 2048, 2048], P('dp', 'context')
- value_grad: bfloat16 [2, 2048, 2048], P('dp', 'context')
- maps_grad: float32 [2048, 128], P(('dp', 'context'))
All inputs are finite; a program needn't handle non-finite values.
Results may differ from a plain program's by a relative error of at most 0.0085.
Values sent between devices are 32-bit elements; how exact they have to be, the bound alone decides.
No kernel may reach another device: no remote copies, remote signals or barrier semaphores. Data moves between devices by JAX's collectives and lax.ppermute only.
A program may use at most 64 MiB of HBM per device.

v0:
```python
import math

import jax
import jax.numpy as jnp
from jax import lax
from jax.sharding import PartitionSpec as P


def block_sums(kv_all, grad_all):
    running_kv = jnp.cumsum(kv_all, axis=0)
    running_grad = jnp.cumsum(grad_all, axis=0)
    before = running_kv - kv_all
    after = running_grad[-1:] - running_grad
    return (before, after)


def split_state(state):
    upper = state.astype(jnp.bfloat16)
    lower = (state - upper.astype(jnp.float32)).astype(jnp.bfloat16)
    return (upper, lower)


def state_product(form, rows, parts):
    return jnp.einsum(form, rows, parts[0], preferred_element_type=jnp.float32) + jnp.einsum(
        form, rows, parts[1], preferred_element_type=jnp.float32
    )


def per_device(queries, key_rows, value_rows, out_grad, feature_maps):
    tokens = queries.shape[1]
    head_count = feature_maps.shape[0]
    head_width = feature_maps.shape[1]
    ranks = lax.axis_size("context")
    length = tokens * ranks
    factor = 1.0 / math.sqrt(head_width * length)
    norm_factor = 1.0 / math.sqrt(lax.axis_size("dp") * length)
    query_heads = queries.reshape(tokens, head_count, head_width)
    key_heads = key_rows.reshape(tokens, head_count, head_width)
    value_heads = value_rows.reshape(tokens, head_count, head_width)
    grad_heads = out_grad.reshape(tokens, head_count, head_width)
    feat_query = jnp.einsum(
        "thd,hde->hte", query_heads, feature_maps, preferred_element_type=jnp.float32
    ).astype(jnp.bfloat16)
    feat_key = jnp.einsum(
        "thd,hde->hte", key_heads, feature_maps, preferred_element_type=jnp.float32
    ).astype(jnp.bfloat16)
    kv_local = jnp.einsum("hsd,she->hde", feat_key, value_heads, preferred_element_type=jnp.float32)
    grad_local = jnp.einsum(
        "htd,the->hde", feat_query, grad_heads, preferred_element_type=jnp.float32
    )
    state_rows = head_count * head_width
    group_rows = state_rows // ranks
    kv_groups = kv_local.reshape(ranks, group_rows, head_width)
    grad_groups = grad_local.reshape(ranks, group_rows, head_width)
    kv_all, grad_all = (
        lax.all_to_all(kv_groups, "context", split_axis=0, concat_axis=0, tiled=True),
        lax.all_to_all(grad_groups, "context", split_axis=0, concat_axis=0, tiled=True),
    )
    before, after = block_sums(kv_all, grad_all)
    before_mine, after_mine = (
        lax.all_to_all(before, "context", split_axis=0, concat_axis=0, tiled=True),
        lax.all_to_all(after, "context", split_axis=0, concat_axis=0, tiled=True),
    )
    prefix_parts = split_state(before_mine.reshape(head_count, head_width, head_width))
    suffix_parts = split_state(after_mine.reshape(head_count, head_width, head_width))
    causal = jnp.arange(tokens)[:, None] >= jnp.arange(tokens)[None, :]
    score_ab = jnp.where(
        causal,
        jnp.einsum("htd,hsd->hts", feat_query, feat_key, preferred_element_type=jnp.float32),
        0.0,
    ).astype(jnp.bfloat16)
    score_gv = jnp.where(
        causal,
        jnp.einsum("the,she->hts", grad_heads, value_heads, preferred_element_type=jnp.float32),
        0.0,
    ).astype(jnp.bfloat16)
    feat_qgrad = factor * (
        jnp.einsum("hts,hsd->htd", score_gv, feat_key, preferred_element_type=jnp.float32)
        + state_product("the,hde->htd", grad_heads, prefix_parts)
    )
    feat_qgrad = feat_qgrad.astype(jnp.bfloat16)
    query_grad = jnp.einsum(
        "hte,hde->thd", feat_qgrad, feature_maps, preferred_element_type=jnp.float32
    )
    query_grad = query_grad.astype(jnp.bfloat16).reshape(1, tokens, head_count * head_width)
    query_term = jnp.einsum(
        "thd,hte->hde", query_heads, feat_qgrad, preferred_element_type=jnp.float32
    )
    feat_kgrad = factor * (
        jnp.einsum("hts,htd->hsd", score_gv, feat_query, preferred_element_type=jnp.float32)
        + state_product("she,hde->hsd", value_heads, suffix_parts)
    )
    feat_kgrad = feat_kgrad.astype(jnp.bfloat16)
    value_grad = factor * (
        jnp.einsum("hts,the->she", score_ab, grad_heads, preferred_element_type=jnp.float32)
        + state_product("hsd,hde->she", feat_key, suffix_parts)
    )
    value_grad = value_grad.astype(jnp.bfloat16).reshape(1, tokens, head_count * head_width)
    key_grad = jnp.einsum(
        "hse,hde->shd", feat_kgrad, feature_maps, preferred_element_type=jnp.float32
    )
    key_grad = key_grad.astype(jnp.bfloat16).reshape(1, tokens, head_count * head_width)
    key_term = jnp.einsum("shd,hse->hde", key_heads, feat_kgrad, preferred_element_type=jnp.float32)
    both_terms = (query_term + key_term).reshape(state_rows, head_width)
    maps_grad = (
        lax.psum_scatter(both_terms, ("dp", "context"), scatter_dimension=0, tiled=True)
        * norm_factor
    )
    return (query_grad, key_grad, value_grad, maps_grad)


def solution(mesh):
    in_specs = (
        P("dp", "context", None),
        P("dp", "context", None),
        P("dp", "context", None),
        P("dp", "context", None),
        P(),
    )
    out_specs = (
        P("dp", "context", None),
        P("dp", "context", None),
        P("dp", "context", None),
        P(("dp", "context"), None),
    )
    return jax.shard_map(
        per_device, mesh=mesh, in_specs=in_specs, out_specs=out_specs, check_vma=False
    )
```

profile of v0, /device:TPU:0, one launch (start us, length us, event | category | flops | bytes accessed | tf_op | source)
XLA Modules:
  0.0 282.0 jit_solution(12650277817571033582)
XLA Ops:
  7.2 1.2 copy.46
  9.5 1.3 fusion.19
  10.9 7.5 %all-to-all-start = ((f32[16,128,128]{2,1,0:T(8,128)}), f32[16,128,128]{2,1,0:T(8,128)S(1)}, u32[]{:S(2)}, u32[]{:S(2)}) async-start(f32[16,128,128]{2,1,0:T(8,128)} %fusion.19), calls=%async_computation | async-start | bytes 2097152 | tf_op jit(solution)/shard_map/all_to_all | solution.py:56
  18.7 2.0 copy.45
  20.7 1.4 convolution_convert_fusion.1
  22.1 1.5 fusion.32
  23.6 17.7 %all-to-all-done = f32[16,128,128]{2,1,0:T(8,128)S(1)} async-done(((f32[16,128,128]{2,1,0:T(8,128)}), f32[16,128,128]{2,1,0:T(8,128)S(1)}, u32[]{:S(2)}, u32[]{:S(2)}) %all-to-all-start) | async-done | bytes 1048608 | tf_op jit(solution)/shard_map/all_to_all | solution.py:56
  41.4 6.9 %all-to-all-start.2 = ((f32[16,128,128]{2,1,0:T(8,128)}), f32[16,128,128]{2,1,0:T(8,128)}, u32[]{:S(2)}, u32[]{:S(2)}) async-start(f32[16,128,128]{2,1,0:T(8,128)} %fusion.32), calls=%async_computation.2 | async-start | bytes 2097152 | tf_op jit(solution)/shard_map/all_to_all | solution.py:57
  48.3 1.1 reduce-window_subtract_fusion
  49.4 21.9 %all-to-all-done.2 = f32[16,128,128]{2,1,0:T(8,128)} async-done(((f32[16,128,128]{2,1,0:T(8,128)}), f32[16,128,128]{2,1,0:T(8,128)}, u32[]{:S(2)}, u32[]{:S(2)}) %all-to-all-start.2) | async-done | bytes 1048608 | tf_op jit(solution)/shard_map/all_to_all | solution.py:57
  71.3 6.9 %all-to-all-start.1 = ((f32[16,128,128]{2,1,0:T(8,128)}), f32[16,128,128]{2,1,0:T(8,128)S(1)}, u32[]{:S(2)}, u32[]{:S(2)}) async-start(f32[16,128,128]{2,1,0:T(8,128)} %reduce-window_subtract_fusion), calls=%async_computation.1 | async-start | bytes 2097152 | tf_op jit(solution)/shard_map/all_to_all | solution.py:61
  78.1 1.3 fusion.29
  79.5 1.1 broadcast_subtract_fusion
  80.5 20.5 %all-to-all-done.1 = f32[16,128,128]{2,1,0:T(8,128)S(1)} async-done(((f32[16,128,128]{2,1,0:T(8,128)}), f32[16,128,128]{2,1,0:T(8,128)S(1)}, u32[]{:S(2)}, u32[]{:S(2)}) %all-to-all-start.1) | async-done | bytes 1048608 | tf_op jit(solution)/shard_map/all_to_all | solution.py:61
  101.1 1.0 copy-done.1
  102.1 6.9 %all-to-all-start.3 = ((f32[16,128,128]{2,1,0:T(8,128)}), f32[16,128,128]{2,1,0:T(8,128)S(1)}, u32[]{:S(2)}, u32[]{:S(2)}) async-start(f32[16,128,128]{2,1,0:T(8,128)} %broadcast_subtract_fusion), calls=%async_computation.3 | async-start | bytes 2097152 | tf_op jit(solution)/shard_map/all_to_all | solution.py:62
  109.0 1.6 fusion.10
  110.6 1.4 fusion.31
  112.2 0.9 copy-done.2
  114.2 0.8 copy-done.8
  115.0 1.3 fusion.33
  116.3 15.6 %all-to-all-done.3 = f32[16,128,128]{2,1,0:T(8,128)S(1)} async-done(((f32[16,128,128]{2,1,0:T(8,128)}), f32[16,128,128]{2,1,0:T(8,128)S(1)}, u32[]{:S(2)}, u32[]{:S(2)}) %all-to-all-start.3) | async-done | bytes 1048608 | tf_op jit(solution)/shard_map/all_to_all | solution.py:62
  131.9 1.6 fusion.17
  134.1 0.5 copy-done.6
  134.9 1.3 convolution_add_fusion
  136.8 1.5 fusion.2
  138.3 1.9 fusion.9
  140.2 1.0 copy.33
  141.7 1.0 copy.32
  143.2 1.0 copy.31
  144.2 129.5 %reduce-scatter.2.cloned.1.call-done = f32[64,128]{1,0:T(8,128)} async-done(((f32[2048,128]{1,0:T(8,128)}), f32[64,128]{1,0:T(8,128)}) %reduce-scatter.2.cloned.1.call-update) | async-done | bytes 32784 | tf_op jit(solution)/shard_map/reduce_scatter | solution.py:106
  273.7 1.4 broadcast_multiply_fusion
  (42 shorter events, 5.2 us)
Async XLA Ops:
  7.2 1.6 copy-start
  7.2 1.3 copy-start.14
  8.4 1.1 copy-start.3
  8.7 0.8 copy-start.5
  10.9 7.5 %copy-start.15 = (bf16[1,128,2048]{2,1,0:T(8,128)(2,1)S(1)}, bf16[1,128,2048]{2,1,0:T(8,128)(2,1)}, u32[]{:S(2)}) copy-start(bf16[1,128,2048]{2,1,0:T(8,128)(2,1)} %param.8) | copy-start | bytes 1572868
  10.9 30.5 %all-to-all-start = ((f32[16,128,128]{2,1,0:T(8,128)}), f32[16,128,128]{2,1,0:T(8,128)S(1)}, u32[]{:S(2)}, u32[]{:S(2)}) async-start(f32[16,128,128]{2,1,0:T(8,128)} %fusion.19), calls=%async_computation | async-start | bytes 2097152 | tf_op jit(solution)/shard_map/all_to_all | solution.py:56
  41.4 29.9 %all-to-all-start.2 = ((f32[16,128,128]{2,1,0:T(8,128)}), f32[16,128,128]{2,1,0:T(8,128)}, u32[]{:S(2)}, u32[]{:S(2)}) async-start(f32[16,128,128]{2,1,0:T(8,128)} %fusion.32), calls=%async_computation.2 | async-start | bytes 2097152 | tf_op jit(solution)/shard_map/all_to_all | solution.py:57
  71.3 29.8 %all-to-all-start.1 = ((f32[16,128,128]{2,1,0:T(8,128)}), f32[16,128,128]{2,1,0:T(8,128)S(1)}, u32[]{:S(2)}, u32[]{:S(2)}) async-start(f32[16,128,128]{2,1,0:T(8,128)} %reduce-window_subtract_fusion), calls=%async_computation.1 | async-start | bytes 2097152 | tf_op jit(solution)/shard_map/all_to_all | solution.py:61
  101.1 1.0 copy-start.1
  102.1 29.8 %all-to-all-start.3 = ((f32[16,128,128]{2,1,0:T(8,128)}), f32[16,128,128]{2,1,0:T(8,128)S(1)}, u32[]{:S(2)}, u32[]{:S(2)}) async-start(f32[16,128,128]{2,1,0:T(8,128)} %broadcast_subtract_fusion), calls=%async_computation.3 | async-start | bytes 2097152 | tf_op jit(solution)/shard_map/all_to_all | solution.py:62
  108.9 164.8 %reduce-scatter.2.cloned.1.call-start = ((), (), s32[]{:S(2)}) async-start(), calls=%async_computation.5 | async-start | bytes 1081344 | tf_op jit(solution)/shard_map/reduce_scatter | solution.py:106
  111.9 1.2 copy-start.2
  113.7 1.3 copy-start.7
  114.2 0.8 copy-start.8
  131.9 1.6 copy-start.4
  131.9 1.7 copy-start.13
  133.5 1.0 copy-start.6
  133.5 1.4 copy-start.12
  134.9 1.3 copy-start.10
  140.1 1.0 copy-start.11
  141.7 1.0 copy-start.9
Sparse Core Ops, SparseCore 0:
  136.4 137.3 reduce-scatter.1
where the time goes:
time: 283 us; the launch traced here: 282 us
  waiting for transfers between devices  205 us (72%)
  starting transfers between devices  28.2 us (10%)
  matrix products  18.4 us (7%)
  between operations  14.3 us (5%)
  local copies, waits for them, and re-layouts  10.9 us (4%)
  other arithmetic  4.85 us (2%)
    reduce_scatter x1, waiting for transfers between devices, per_device(): lax.psum_scatter(both_terms, ('dp', 'context'), scatter_dimension=0, tile...  130 us
    all_to_all x1, waiting for transfers between devices, per_device(): lax.all_to_all(grad_groups, 'context', split_axis=0, concat_axis=0, tiled...  21.9 us
    all_to_all x1, waiting for transfers between devices, per_device(): lax.all_to_all(before, 'context', split_axis=0, concat_axis=0, tiled=True)  20.5 us
    all_to_all x1, waiting for transfers between devices, per_device(): lax.all_to_all(kv_groups, 'context', split_axis=0, concat_axis=0, tiled=T...  17.7 us
    all_to_all x1, waiting for transfers between devices, per_device(): lax.all_to_all(after, 'context', split_axis=0, concat_axis=0, tiled=True)  15.6 us
    unnamed x36, local copies, waits for them, and re-layouts  8.33 us
    all_to_all x1, starting transfers between devices, per_device(): lax.all_to_all(kv_groups, 'context', split_axis=0, concat_axis=0, tiled=T...  7.52 us
    all_to_all x1, starting transfers between devices, per_device(): lax.all_to_all(grad_groups, 'context', split_axis=0, concat_axis=0, tiled...  6.92 us
  transfers between devices with their start and end apart: 5, of which 5 were waited for; matrix products, arithmetic and copies ran while one was open for 8% of the time, Pallas kernels for 0%

commit v1 on v0

v1 whole, which is shorter than its diff:
```python
import functools
import math

import jax
import jax.numpy as jnp
from jax import lax
from jax.experimental import pallas as pl
from jax.experimental.pallas import tpu as pltpu
from jax.sharding import PartitionSpec as P

F32 = jnp.float32
BF16 = jnp.bfloat16
VMEM_LIMIT = 32 * 1024 * 1024


class Plan:
    def __init__(self, heads, width, tokens, ranks, copies):
        self.heads, self.width, self.tokens = heads, width, tokens
        self.ranks, self.copies = ranks, copies
        self.groups = ranks // 4
        per_copy = heads // copies if heads % copies == 0 else 0
        self.chunks = 2 if per_copy and per_copy % 2 == 0 and self.groups % 2 == 0 else 1
        self.in_chunk = heads // self.chunks
        self.half = self.in_chunk // 2
        self.run = per_copy // self.chunks if self.chunks > 1 else self.in_chunk
        self.stride = per_copy if self.chunks > 1 else 0
        self.factor = 1.0 / math.sqrt(width * tokens * ranks)
        self.norm = 1.0 / math.sqrt(copies * tokens * ranks)

    def head(self, chunk, place):
        return (place // self.run) * self.stride + chunk * self.run + place % self.run


def device_place():
    index = lax.axis_index("context")
    return index % 2, (index // 2) % 2, index // 4


def columns(ref, head, width):
    start = head * width
    if not isinstance(start, int):
        start = pl.multiple_of(start, width)
    return ref[:, pl.ds(start, width)]


def dot(left, right, left_dim=1, right_dim=0):
    return lax.dot_general(
        left, right, (((left_dim,), (right_dim,)), ((), ())), preferred_element_type=F32
    )


def state_dot(rows, state, state_dim):
    upper = state.astype(BF16)
    lower = (state - upper.astype(F32)).astype(BF16)
    return dot(rows, upper, 1, state_dim) + dot(rows, lower, 1, state_dim)


def by_core(core, zero, one):
    pl.when(core == 0)(zero)
    pl.when(core == 1)(one)


def call(body, operands, shapes, flops):
    moved = sum(x.size * x.dtype.itemsize for x in list(operands) + list(shapes))
    return pl.pallas_call(
        body,
        out_shape=shapes,
        in_specs=[pl.BlockSpec(memory_space=pltpu.VMEM)] * len(operands),
        out_specs=[pl.BlockSpec(memory_space=pltpu.VMEM)] * len(shapes),
        compiler_params=pltpu.CompilerParams(vmem_limit_bytes=VMEM_LIMIT),
        cost_estimate=pl.CostEstimate(flops=flops, bytes_accessed=moved, transcendentals=0),
    )(*operands)


def matmuls(plan, count):
    return 2 * count * plan.tokens * plan.width * plan.width


def states_kernel(plan, own, q_ref, k_ref, v_ref, g_ref, maps_ref, *out_refs):
    core, chip, _ = device_place()

    def fill(rows_ref, with_ref):
        for chunk in range(plan.chunks):
            for part in range(2):
                first = jnp.where(chip == part, 0, plan.half)
                for i in range(plan.half):
                    head = plan.head(chunk, first + i)
                    feat = dot(columns(rows_ref, head, plan.width), maps_ref[head]).astype(BF16)
                    out_refs[2 * chunk + part][i] = dot(
                        feat, columns(with_ref, head, plan.width), 0, 0
                    )

    keys = lambda: fill(k_ref, v_ref)
    queries = lambda: fill(q_ref, g_ref)
    if own:
        by_core(core, queries, keys)
    else:
        by_core(core, keys, queries)


def states(plan, own, rows, maps):
    shape = jax.ShapeDtypeStruct((plan.half, plan.width, plan.width), F32)
    outs = call(
        functools.partial(states_kernel, plan, own),
        (*rows, maps),
        [shape] * (2 * plan.chunks),
        matmuls(plan, 2 * plan.heads),
    )
    return [outs[2 * chunk : 2 * chunk + 2] for chunk in range(plan.chunks)]


def inner_kernel(plan, q_ref, k_ref, v_ref, g_ref, maps_ref, *out_refs):
    tokens, width = plan.tokens, plan.width
    row = lax.broadcasted_iota(jnp.int32, (tokens, tokens), 0)
    column = lax.broadcasted_iota(jnp.int32, (tokens, tokens), 1)
    causal = row >= column
    for chunk in range(plan.chunks):
        feat_ref, da_ref, db_ref, dv_ref = out_refs[4 * chunk : 4 * chunk + 4]
        for place in range(plan.in_chunk):
            head = plan.head(chunk, place)
            grads, values = columns(g_ref, head, width), columns(v_ref, head, width)
            feat_query = dot(columns(q_ref, head, width), maps_ref[head]).astype(BF16)
            feat_key = dot(columns(k_ref, head, width), maps_ref[head]).astype(BF16)
            score_gv = jnp.where(causal, dot(grads, values, 1, 1), 0.0).astype(BF16)
            score_ab = jnp.where(causal, dot(feat_query, feat_key, 1, 1), 0.0).astype(BF16)
            feat_ref[place] = feat_key
            da_ref[place] = dot(score_gv, feat_key)
            db_ref[place] = dot(score_gv, feat_query, 0, 0)
            dv_ref[place] = dot(score_ab, grads, 0, 0)


def inner(plan, rows, maps):
    wide = jax.ShapeDtypeStruct((plan.in_chunk, plan.tokens, plan.width), F32)
    narrow = jax.ShapeDtypeStruct((plan.in_chunk, plan.tokens, plan.width), BF16)
    outs = call(
        functools.partial(inner_kernel, plan),
        (*rows, maps),
        [narrow, wide, wide, wide] * plan.chunks,
        matmuls(plan, 7 * plan.heads),
    )
    return [outs[4 * chunk : 4 * chunk + 4] for chunk in range(plan.chunks)]


def query_side(plan, head, place, state, q_ref, g_ref, da_ref):
    total = da_ref[place] + state_dot(columns(g_ref, head, plan.width), state, 1)
    grad = (plan.factor * total).astype(BF16)
    return grad, dot(columns(q_ref, head, plan.width), grad, 0, 0)


def key_side(plan, head, place, state, k_ref, v_ref, feat_ref, db_ref, dv_ref):
    total = db_ref[place] + state_dot(columns(v_ref, head, plan.width), state, 1)
    grad = (plan.factor * total).astype(BF16)
    values = plan.factor * (dv_ref[place] + state_dot(feat_ref[place], state, 0))
    return grad, dot(columns(k_ref, head, plan.width), grad, 0, 0), values.astype(BF16)


def outer_kernel(plan, own, chunk, *refs):
    core, chip, _ = device_place()
    q_ref, k_ref, v_ref, g_ref, feat_ref, da_ref, db_ref, dv_ref, keep_ref, give_ref = refs[:10]
    extra, (grad_ref, term_ref, value_ref) = refs[10:-3], refs[-3:]

    def each(use):
        for part, state_ref in enumerate((keep_ref, give_ref)):
            first = jnp.where(chip == part, 0, plan.half)
            for i in range(plan.half):
                place = first + i
                state = state_ref[i]
                if own:
                    state = state + extra[part][i]
                use(plan.head(chunk, place), place, state)

    def put(place, grad, term):
        grad_ref[place] = grad
        term_ref[place] = term if own else term + extra[0][place]

    def use_queries(head, place, state):
        put(place, *query_side(plan, head, place, state, q_ref, g_ref, da_ref))

    def use_keys(head, place, state):
        grad, term, values = key_side(
            plan, head, place, state, k_ref, v_ref, feat_ref, db_ref, dv_ref
        )
        put(place, grad, term)
        value_ref[place] = values

    queries, keys = lambda: each(use_queries), lambda: each(use_keys)
    if own:
        by_core(core, keys, queries)
    else:
        by_core(core, queries, keys)


def outer(plan, own, chunk, rows, stash, keep, give, extra):
    shape = (plan.in_chunk, plan.tokens, plan.width)
    square = (plan.in_chunk, plan.width, plan.width)
    return call(
        functools.partial(outer_kernel, plan, own, chunk),
        (*rows, *stash, keep, give, *extra),
        [
            jax.ShapeDtypeStruct(shape, BF16),
            jax.ShapeDtypeStruct(square, F32),
            jax.ShapeDtypeStruct(shape, BF16),
        ],
        matmuls(plan, 5 * plan.in_chunk),
    )


def rows_kernel(plan, maps_ref, *refs):
    core, _, _ = device_place()
    qg_ref, kg_ref, vg_ref = refs[-3:]

    def fill(order):
        for chunk in range(plan.chunks):
            own_grad, own_value, far_grad, far_value = refs[4 * chunk : 4 * chunk + 4]
            da_ref, db_ref, dv_ref = (
                (own_grad, far_grad, far_value) if order else (far_grad, own_grad, own_value)
            )
            for place in range(plan.in_chunk):
                head = plan.head(chunk, place)
                at = pl.ds(head * plan.width, plan.width)
                qg_ref[:, at] = dot(da_ref[place], maps_ref[head], 1, 1).astype(BF16)
                kg_ref[:, at] = dot(db_ref[place], maps_ref[head], 1, 1).astype(BF16)
                vg_ref[:, at] = dv_ref[place]

    by_core(core, lambda: fill(0), lambda: fill(1))


def output_rows(plan, maps, pieces):
    shape = jax.ShapeDtypeStruct((plan.tokens, plan.heads * plan.width), BF16)
    return call(
        functools.partial(rows_kernel, plan),
        (maps, *pieces),
        [shape] * 3,
        matmuls(plan, 2 * plan.heads),
    )


def swap_core(plan, state):
    return lax.ppermute(state, "context", [(i, i ^ 1) for i in range(plan.ranks)])


def swap_chip(plan, state):
    return lax.ppermute(state, "context", [(i, i ^ 2) for i in range(plan.ranks)])


def chain_hop(plan, state, hop):
    steps = []
    for low in range(4):
        source = hop if low % 2 else plan.groups - 1 - hop
        target = source + (1 if low % 2 else -1)
        steps.append((4 * source + low, 4 * target + low))
    return lax.ppermute(state, "context", steps)


def plane_sums(plan, terms):
    core, chip, _ = device_place()
    replica = lax.axis_index("dp")
    ranks, copies, width = plan.ranks, plan.copies, plan.width
    height = plan.heads * width // (copies * ranks)
    parts = terms.reshape(-1, 2, height, width)
    sent = lax.dynamic_index_in_dim(parts, 1 - core, 1, keepdims=False)
    kept = lax.dynamic_index_in_dim(parts, core, 1, keepdims=False)
    total = (kept + swap_core(plan, sent)).reshape(copies, -1, 2, height, width)

    def plane_part(target_replica, target_chip):
        some = lax.dynamic_index_in_dim(total, target_replica, 0, keepdims=False)
        return lax.dynamic_index_in_dim(some, target_chip, 1, keepdims=False)

    plane = plane_part(replica, chip)
    for turn in range(copies):
        for flip in range(2):
            if turn == 0 and flip == 0:
                continue
            steps = [
                (r * ranks + i, ((r + turn) % copies) * ranks + (i ^ (2 * flip)))
                for r in range(copies)
                for i in range(ranks)
            ]
            sent = plane_part((replica + turn) % copies, (chip + flip) % 2)
            plane = plane + lax.ppermute(sent, ("dp", "context"), steps)
    return plane


def group_sum(plan, plane):
    _, _, group = device_place()
    result = lax.dynamic_index_in_dim(plane, group, 0, keepdims=False)
    for turn in range(1, plan.groups):
        steps = [(i, (i + 4 * turn) % plan.ranks) for i in range(plan.ranks)]
        sent = lax.dynamic_index_in_dim(plane, (group + turn) % plan.groups, 0, keepdims=False)
        result = result + lax.ppermute(sent, "context", steps)
    return result


def per_device(queries, key_rows, value_rows, out_grad, feature_maps):
    tokens = queries.shape[1]
    heads, width, _ = feature_maps.shape
    plan = Plan(heads, width, tokens, lax.axis_size("context"), lax.axis_size("dp"))
    rows = [x.reshape(tokens, heads * width) for x in (queries, key_rows, value_rows, out_grad)]
    core, chip, _ = device_place()
    last = chip == core
    chunks = range(plan.chunks)

    sent = states(plan, False, rows, feature_maps)
    from_core = [[swap_core(plan, x) for x in sent[chunk]] for chunk in chunks]
    mine = states(plan, True, rows, feature_maps)
    stash = inner(plan, rows, feature_maps)

    kept, from_chip, group = [], [], []
    for chunk in chunks:
        given = mine[chunk][1] + from_core[chunk][1]
        if chunk:
            given, from_chip[-1] = lax.optimization_barrier((given, from_chip[-1]))
        kept.append(mine[chunk][0] + from_core[chunk][0])
        from_chip.append(swap_chip(plan, given))
        group.append(kept[chunk] + from_chip[chunk])

    before = [jnp.zeros_like(x) for x in group]
    for stage in range(plan.groups - 1 + plan.chunks - 1):
        for chunk in chunks:
            hop = stage - chunk
            if 0 <= hop < plan.groups - 1:
                before[chunk] = before[chunk] + chain_hop(plan, before[chunk] + group[chunk], hop)

    planes, pieces = [], []
    for chunk in chunks:
        keep = before[chunk] + jnp.where(last, from_chip[chunk], 0.0)
        give = swap_chip(plan, before[chunk] + jnp.where(last, 0.0, kept[chunk]))
        far_keep, far_give = swap_core(plan, keep), swap_core(plan, give)
        grad, term, value = outer(
            plan, True, chunk, rows, stash[chunk], keep, give, from_core[chunk]
        )
        far_grad, term, far_value = outer(
            plan, False, chunk, rows, stash[chunk], far_keep, far_give, [term]
        )
        pieces += [grad, value, far_grad, far_value]
        planes.append(plane_sums(plan, term))
    query_grad, key_grad, value_grad = output_rows(plan, feature_maps, pieces)
    maps_grad = group_sum(plan, jnp.concatenate(planes, axis=0)) * plan.norm
    return (query_grad[None], key_grad[None], value_grad[None], maps_grad)


def solution(mesh):
    in_specs = (
        P("dp", "context", None),
        P("dp", "context", None),
        P("dp", "context", None),
        P("dp", "context", None),
        P(),
    )
    out_specs = (
        P("dp", "context", None),
        P("dp", "context", None),
        P("dp", "context", None),
        P(("dp", "context"), None),
    )
    return jax.shard_map(
        per_device, mesh=mesh, in_specs=in_specs, out_specs=out_specs, check_vma=False
    )
```

time: 283 us -> 101 us (0.36)
  waiting for transfers between devices: 205 us -> 31.6 us
  Pallas kernels: 0 us -> 20.5 us
  matrix products: 18.4 us -> 0 us
  between operations: 14.3 us -> 1.21 us
  local copies, waits for them, and re-layouts: 10.9 us -> 16.1 us
    reduce_scatter x1 -> x0, waiting for transfers between devices: 130 us -> none  [per_device(): lax.psum_scatter(both_terms, ('dp', 'context'), scatter_dimension=0, tile...]
    all_to_all x4 -> x0, waiting for transfers between devices: 75.8 us -> none  [the longest x1 21.9 us: per_device(): lax.all_to_all(grad_groups, 'context', split_axis=0, concat_axis=0, tiled...]
    ppermute x0 -> x29, waiting for transfers between devices: none -> 31.6 us  [the longest x6 15.4 us: chain_hop(): return lax.ppermute(state, 'context', steps)]
    all_to_all x4 -> x0, starting transfers between devices: 28.2 us -> none  [the longest x1 7.52 us: per_device(): lax.all_to_all(kv_groups, 'context', split_axis=0, concat_axis=0, tiled=T...]
    ppermute x0 -> x29, starting transfers between devices: none -> 26.9 us  [the longest x4 7.74 us: swap_chip(): lax.ppermute(state, 'context', [(i, i ^ 2) for i in range(plan.ranks)])]
    pallas_call x0 -> x8, Pallas kernels: none -> 20.5 us  [call(): pl.pallas_call(body, out_shape=shapes, in_specs=[pl.BlockSpec(memory_spac...]
    dot_general x18 -> x0, matrix products: 18.4 us -> none  [the longest x3 2.67 us: state_product(): jnp.einsum(form, rows, parts[0], preferred_element_type=jnp.float32)]
    unnamed x36 -> x84, local copies, waits for them, and re-layouts: 8.33 us -> 15.2 us
  transfers between devices with their start and end apart: 5 -> 29, of which waited for: 5 -> 9; matrix products, arithmetic and copies ran while one was open for 8% -> 4% of each run, Pallas kernels for 0% -> 20%
where the time goes in v1:
time: 101 us; the launch traced here: 99.9 us
  waiting for transfers between devices  31.6 us (31%)
  starting transfers between devices  26.9 us (27%)
  Pallas kernels  20.5 us (20%)
  local copies, waits for them, and re-layouts  16.1 us (16%)
  other arithmetic  3.64 us (4%)
  between operations  1.21 us (1%)
    pallas_call x8, Pallas kernels, call(): pl.pallas_call(body, out_shape=shapes, in_specs=[pl.BlockSpec(memory_spac...  20.5 us
    ppermute x6, waiting for transfers between devices, chain_hop(): return lax.ppermute(state, 'context', steps)  15.4 us
    unnamed x84, local copies, waits for them, and re-layouts  15.2 us
    ppermute x4, waiting for transfers between devices, swap_chip(): lax.ppermute(state, 'context', [(i, i ^ 2) for i in range(plan.ranks)])  10.7 us
    ppermute x4, starting transfers between devices, swap_chip(): lax.ppermute(state, 'context', [(i, i ^ 2) for i in range(plan.ranks)])  7.74 us
    ppermute x6, starting transfers between devices, plane_sums(): plane = plane + lax.ppermute(sent, ('dp', 'context'), steps)  7.11 us
    ppermute x6, starting transfers between devices, chain_hop(): return lax.ppermute(state, 'context', steps)  5.29 us
    ppermute x3, starting transfers between devices, group_sum(): result = result + lax.ppermute(sent, 'context', steps)  4.27 us
  transfers between devices with their start and end apart: 29, of which 9 were waited for; matrix products, arithmetic and copies ran while one was open for 4% of the time, Pallas kernels for 20%

profile of v1, /device:TPU:0, one launch (start us, length us, event | category | flops | bytes accessed | tf_op | source)
XLA Modules:
  0.0 99.9 jit_solution(18258293581250904421)
XLA Ops:
  0.6 1.0 %copy-done = bf16[1,128,2048]{2,1,0:T(8,128)(2,1)S(1)} copy-done((bf16[1,128,2048]{2,1,0:T(8,128)(2,1)S(1)}, bf16[1,128,2048]{2,1,0:T(8,128)(2,1)}, u32[]{:S(2)}) %copy-start) | copy-done | bytes 524312
  1.7 1.0 %copy-done.2 = bf16[1,128,2048]{2,1,0:T(8,128)(2,1)S(1)} copy-done((bf16[1,128,2048]{2,1,0:T(8,128)(2,1)S(1)}, bf16[1,128,2048]{2,1,0:T(8,128)(2,1)}, u32[]{:S(2)}) %copy-start.2) | copy-done | bytes 524312
  2.7 1.0 %copy-done.4 = bf16[1,128,2048]{2,1,0:T(8,128)(2,1)S(1)} copy-done((bf16[1,128,2048]{2,1,0:T(8,128)(2,1)S(1)}, bf16[1,128,2048]{2,1,0:T(8,128)(2,1)}, u32[]{:S(2)}) %copy-start.4) | copy-done | bytes 524312
  3.8 1.0 %copy-done.6 = bf16[1,128,2048]{2,1,0:T(8,128)(2,1)S(1)} copy-done((bf16[1,128,2048]{2,1,0:T(8,128)(2,1)S(1)}, bf16[1,128,2048]{2,1,0:T(8,128)(2,1)}, u32[]{:S(2)}) %copy-start.6) | copy-done | bytes 524312
  4.8 1.0 %copy-done.8 = bf16[16,128,128]{2,1,0:T(8,128)(2,1)S(1)} copy-done((bf16[16,128,128]{2,1,0:T(8,128)(2,1)S(1)}, bf16[16,128,128]{2,1,0:T(8,128)(2,1)}, u32[]{:S(2)}) %copy-start.8) | copy-done | bytes 524312
  8.1 3.0 %collective-permute-start.2 = (f32[4,128,128]{2,1,0:T(8,128)S(1)}, f32[4,128,128]{2,1,0:T(8,128)S(1)}, u32[]{:S(2)}, u32[]{:S(2)}) collective-permute-start(f32[4,128,128]{2,1,0:T(8,128)S(1)} %add.244), channel_id=1, source_target_pairs={{0,2},{1,3},{2,0},{3,1},{4,6},{5,7},{6,4},{7,5},{8,10},{9,11},{10,... | collective-permute-start | bytes 786440 | tf_op jit(solution)/shard_map/ppermute | solution.py:243
  12.3 5.4 %collective-permute-done.2 = f32[4,128,128]{2,1,0:T(8,128)S(1)} collective-permute-done((f32[4,128,128]{2,1,0:T(8,128)S(1)}, f32[4,128,128]{2,1,0:T(8,128)S(1)}, u32[]{:S(2)}, u32[]{:S(2)}) %collective-permute-start.2) | collective-permute-done | bytes 262176 | tf_op jit(solution)/shard_map/ppermute | solution.py:243
  17.7 1.7 %collective-permute-start.11 = (f32[4,128,128]{2,1,0:T(8,128)S(1)}, f32[4,128,128]{2,1,0:T(8,128)S(1)}, u32[]{:S(2)}, u32[]{:S(2)}) collective-permute-start(f32[4,128,128]{2,1,0:T(8,128)S(1)} %add.252), channel_id=1, source_target_pairs={{0,2},{1,3},{2,0},{3,1},{4,6},{5,7},{6,4},{7,5},{8,10},{9,11},{10,... | collective-permute-start | bytes 786440 | tf_op jit(solution)/shard_map/ppermute | solution.py:243
  20.2 5.3 %collective-permute-done.11 = f32[4,128,128]{2,1,0:T(8,128)S(1)} collective-permute-done((f32[4,128,128]{2,1,0:T(8,128)S(1)}, f32[4,128,128]{2,1,0:T(8,128)S(1)}, u32[]{:S(2)}, u32[]{:S(2)}) %collective-permute-start.11) | collective-permute-done | bytes 262176 | tf_op jit(solution)/shard_map/ppermute | solution.py:243
  28.5 1.3 %collective-permute-start.5 = (f32[4,128,128]{2,1,0:T(8,128)S(1)}, f32[4,128,128]{2,1,0:T(8,128)S(1)}, u32[]{:S(2)}, u32[]{:S(2)}) collective-permute-start(f32[4,128,128]{2,1,0:T(8,128)S(1)} %get-tuple-element.72), channel_id=1, source_target_pairs={{4,0},{9,13},{6,2},{11,15},{20,16},{25,29},{22,18},{27,31}} | collective-permute-start | bytes 786440 | tf_op jit(solution)/shard_map/ppermute | solution.py:252
  29.9 1.3 %collective-permute-start.14 = (f32[4,128,128]{2,1,0:T(8,128)S(1)}, f32[4,128,128]{2,1,0:T(8,128)S(1)}, u32[]{:S(2)}, u32[]{:S(2)}) collective-permute-start(f32[4,128,128]{2,1,0:T(8,128)S(1)} %get-tuple-element.70), channel_id=1, source_target_pairs={{4,0},{9,13},{6,2},{11,15},{20,16},{25,29},{22,18},{27,31}} | collective-permute-start | bytes 786440 | tf_op jit(solution)/shard_map/ppermute | solution.py:252
  31.2 11.2 %collective-permute-done.5 = f32[4,128,128]{2,1,0:T(8,128)S(1)} collective-permute-done((f32[4,128,128]{2,1,0:T(8,128)S(1)}, f32[4,128,128]{2,1,0:T(8,128)S(1)}, u32[]{:S(2)}, u32[]{:S(2)}) %collective-permute-start.5) | collective-permute-done | bytes 262176 | tf_op jit(solution)/shard_map/ppermute | solution.py:252
  43.3 1.5 %collective-permute-start.7 = (f32[4,128,128]{2,1,0:T(8,128)S(1)}, f32[4,128,128]{2,1,0:T(8,128)}, u32[]{:S(2)}, u32[]{:S(2)}) collective-permute-start(f32[4,128,128]{2,1,0:T(8,128)S(1)} %get-tuple-element.76), channel_id=1, source_target_pairs={{0,2},{1,3},{2,0},{3,1},{4,6},{5,7},{6,4},{7,5},{8,10},{9,11},{10,... | collective-permute-start | bytes 786440 | tf_op jit(solution)/shard_map/ppermute | solution.py:243
  44.8 4.2 %collective-permute-done.14 = f32[4,128,128]{2,1,0:T(8,128)S(1)} collective-permute-done((f32[4,128,128]{2,1,0:T(8,128)S(1)}, f32[4,128,128]{2,1,0:T(8,128)S(1)}, u32[]{:S(2)}, u32[]{:S(2)}) %collective-permute-start.14) | collective-permute-done | bytes 262176 | tf_op jit(solution)/shard_map/ppermute | solution.py:252
  49.8 1.5 %collective-permute-start.15 = (f32[4,128,128]{2,1,0:T(8,128)}, f32[4,128,128]{2,1,0:T(8,128)}, u32[]{:S(2)}, u32[]{:S(2)}) collective-permute-start(f32[4,128,128]{2,1,0:T(8,128)} %get-tuple-element.74), channel_id=1, source_target_pairs={{0,2},{1,3},{2,0},{3,1},{4,6},{5,7},{6,4},{7,5},{8,10},{9,11},{10,... | collective-permute-start | bytes 786440 | tf_op jit(solution)/shard_map/ppermute | solution.py:243
  51.9 5.6 %shard_map.84 = (bf16[8,128,128]{2,1,0:T(8,128)(2,1)S(1)}, f32[8,128,128]{2,1,0:T(8,128)S(1)}, f32[8,128,128]{2,1,0:T(8,128)S(1)}, f32[8,128,128]{2,1,0:T(8,128)...) custom-call(bf16[128,2048]{1,0:T(8,128)(2,1)S(1)} %bitcast.61, ...), custom_call_target="tpu_custom_call" | custom-call | flops 469762048 | bytes 6291456 | tf_op jit(solution)/shard_map/pallas_call | solution.py:65
  59.8 3.1 %shard_map.87 = (bf16[8,128,128]{2,1,0:T(8,128)(2,1)S(1)}, f32[8,128,128]{2,1,0:T(8,128)S(1)}, bf16[8,128,128]{2,1,0:T(8,128)(2,1)S(1)}) custom-call(bf16[128,2048]{1,0:T(8,128)(2,1)S(1)} %bitcast.62, bf16[128,2048]{1,0:T(8,128)(2,1)S(1)} %bitcast.69, bf16[128,2048]{1,0:T(8,128)(2,1)S(1)} %bitcast.76, bf16[128,2048]{1,0:T(8,128)(2,1)S(1)} %bitcast.83, ...), custom_call_target="tpu_custom_call" | custom-call | flops 167772160 | bytes 6029312 | tf_op jit(solution)/shard_map/pallas_call | solution.py:65
  63.2 2.9 %shard_map.88 = (bf16[8,128,128]{2,1,0:T(8,128)(2,1)S(1)}, f32[8,128,128]{2,1,0:T(8,128)S(1)}, bf16[8,128,128]{2,1,0:T(8,128)(2,1)S(1)}) custom-call(bf16[128,2048]{1,0:T(8,128)(2,1)S(1)} %bitcast.63, bf16[128,2048]{1,0:T(8,128)(2,1)S(1)} %bitcast.70, bf16[128,2048]{1,0:T(8,128)(2,1)S(1)} %bitcast.77, bf16[128,2048]{1,0:T(8,128)(2,1)S(1)} %bitcast.84, ...), custom_call_target="tpu_custom_call" | custom-call | flops 167772160 | bytes 6029312 | tf_op jit(solution)/shard_map/pallas_call | solution.py:65
  67.9 1.0 %copy-done.13 = f32[8,128,128]{2,1,0:T(8,128)S(1)} copy-done((f32[8,128,128]{2,1,0:T(8,128)S(1)}, f32[8,128,128]{2,1,0:T(8,128)}, u32[]{:S(2)}) %copy-start.13) | copy-done | bytes 524312
  69.0 1.0 %copy-done.15 = f32[8,128,128]{2,1,0:T(8,128)S(1)} copy-done((f32[8,128,128]{2,1,0:T(8,128)S(1)}, f32[8,128,128]{2,1,0:T(8,128)}, u32[]{:S(2)}) %copy-start.15) | copy-done | bytes 524312
  71.9 2.9 %shard_map.89 = (bf16[8,128,128]{2,1,0:T(8,128)(2,1)S(1)}, f32[8,128,128]{2,1,0:T(8,128)S(1)}, bf16[8,128,128]{2,1,0:T(8,128)(2,1)S(1)}) custom-call(bf16[128,2048]{1,0:T(8,128)(2,1)S(1)} %bitcast.64, bf16[128,2048]{1,0:T(8,128)(2,1)S(1)} %bitcast.71, bf16[128,2048]{1,0:T(8,128)(2,1)S(1)} %bitcast.78, bf16[128,2048]{1,0:T(8,128)(2,1)S(1)} %bitcast.85, ...), custom_call_target="tpu_custom_call" | custom-call | flops 167772160 | bytes 6029312 | tf_op jit(solution)/shard_map/pallas_call | solution.py:65
  75.5 2.9 %shard_map.90 = (bf16[8,128,128]{2,1,0:T(8,128)(2,1)S(1)}, f32[8,128,128]{2,1,0:T(8,128)S(1)}, bf16[8,128,128]{2,1,0:T(8,128)(2,1)S(1)}) custom-call(bf16[128,2048]{1,0:T(8,128)(2,1)S(1)} %bitcast.65, bf16[128,2048]{1,0:T(8,128)(2,1)S(1)} %bitcast.72, bf16[128,2048]{1,0:T(8,128)(2,1)S(1)} %bitcast.79, bf16[128,2048]{1,0:T(8,128)(2,1)S(1)} %bitcast.86, ...), custom_call_target="tpu_custom_call" | custom-call | flops 167772160 | bytes 6029312 | tf_op jit(solution)/shard_map/pallas_call | solution.py:65
  79.6 1.0 bitcast_add_fusion.1
  80.6 1.5 %collective-permute-start.21 = (f32[2,64,128]{2,1,0:T(8,128)S(1)}, f32[2,64,128]{2,1,0:T(8,128)S(1)}, u32[]{:S(2)}, u32[]{:S(2)}) collective-permute-start(f32[2,64,128]{2,1,0:T(8,128)S(1)} %get-tuple-element.82), channel_id=1, source_target_pairs={{0,18},{1,19},{2,16},{3,17},{4,22},{5,23},{6,20},{7,21},{8,26},{9,... | collective-permute-start | bytes 196616 | tf_op jit(solution)/shard_map/ppermute | solution.py:280
  82.7 1.5 %collective-permute-start.19 = (f32[2,64,128]{2,1,0:T(8,128)S(1)}, f32[2,64,128]{2,1,0:T(8,128)S(1)}, u32[]{:S(2)}, u32[]{:S(2)}) collective-permute-start(f32[2,64,128]{2,1,0:T(8,128)S(1)} %get-tuple-element.81), channel_id=1, source_target_pairs={{0,2},{1,3},{2,0},{3,1},{4,6},{5,7},{6,4},{7,5},{8,10},{9,11},{10,... | collective-permute-start | bytes 196616 | tf_op jit(solution)/shard_map/ppermute | solution.py:280
  84.3 1.5 %collective-permute-start.25 = (f32[2,64,128]{2,1,0:T(8,128)S(1)}, f32[2,64,128]{2,1,0:T(8,128)S(1)}, u32[]{:S(2)}, u32[]{:S(2)}) collective-permute-start(f32[2,64,128]{2,1,0:T(8,128)S(1)} %get-tuple-element.79), channel_id=1, source_target_pairs={{0,18},{1,19},{2,16},{3,17},{4,22},{5,23},{6,20},{7,21},{8,26},{9,... | collective-permute-start | bytes 196616 | tf_op jit(solution)/shard_map/ppermute | solution.py:280
  86.3 1.5 %collective-permute-start.23 = (f32[2,64,128]{2,1,0:T(8,128)S(1)}, f32[2,64,128]{2,1,0:T(8,128)S(1)}, u32[]{:S(2)}, u32[]{:S(2)}) collective-permute-start(f32[2,64,128]{2,1,0:T(8,128)S(1)} %get-tuple-element.78), channel_id=1, source_target_pairs={{0,2},{1,3},{2,0},{3,1},{4,6},{5,7},{6,4},{7,5},{8,10},{9,11},{10,... | collective-permute-start | bytes 196616 | tf_op jit(solution)/shard_map/ppermute | solution.py:280
  87.9 1.9 %collective-permute-done.25 = f32[2,64,128]{2,1,0:T(8,128)S(1)} collective-permute-done((f32[2,64,128]{2,1,0:T(8,128)S(1)}, f32[2,64,128]{2,1,0:T(8,128)S(1)}, u32[]{:S(2)}, u32[]{:S(2)}) %collective-permute-start.25) | collective-permute-done | bytes 65568 | tf_op jit(solution)/shard_map/ppermute | solution.py:280
  90.7 2.8 %collective-permute-start.27 = (f32[64,128]{1,0:T(8,128)S(1)}, f32[64,128]{1,0:T(8,128)S(1)}, u32[]{:S(2)}, u32[]{:S(2)}) collective-permute-start(f32[64,128]{1,0:T(8,128)S(1)} %get-tuple-element.85), channel_id=1, source_target_pairs={{0,8},{1,9},{2,10},{3,11},{4,12},{5,13},{6,14},{7,15},{8,0},{9,1},... | collective-permute-start | bytes 98312 | tf_op jit(solution)/shard_map/ppermute | solution.py:290
  93.6 1.3 %collective-permute-start.26 = (f32[64,128]{1,0:T(8,128)S(1)}, f32[64,128]{1,0:T(8,128)S(1)}, u32[]{:S(2)}, u32[]{:S(2)}) collective-permute-start(f32[64,128]{1,0:T(8,128)S(1)} %get-tuple-element.84), channel_id=1, source_target_pairs={{0,4},{1,5},{2,6},{3,7},{4,8},{5,9},{6,10},{7,11},{8,12},{9,13},{1... | collective-permute-start | bytes 98312 | tf_op jit(solution)/shard_map/ppermute | solution.py:290
  95.0 2.1 %shard_map.91 = (bf16[128,2048]{1,0:T(8,128)(2,1)}, bf16[128,2048]{1,0:T(8,128)(2,1)}, bf16[128,2048]{1,0:T(8,128)(2,1)}) custom-call(bf16[16,128,128]{2,1,0:T(8,128)(2,1)S(1)} %copy-done.9, bf16[8,128,128]{2,1,0:T(8,128)(2,1)S(1)} %copy-done.25, bf16[8,128,128]{2,1,0:T(8,128)(2,1)S(1)} %copy-done.27, bf16[8,128,128]{2,1,0:T(8,128)(2,1)S(1)} %copy-done.29, ...), custom_call_target="tpu_custom_call" | custom-call | flops 134217728 | bytes 4194304 | tf_op jit(solution)/shard_map/pallas_call | solution.py:65
  97.0 2.3 %collective-permute-done.26 = f32[64,128]{1,0:T(8,128)S(1)} collective-permute-done((f32[64,128]{1,0:T(8,128)S(1)}, f32[64,128]{1,0:T(8,128)S(1)}, u32[]{:S(2)}, u32[]{:S(2)}) %collective-permute-start.26) | collective-permute-done | bytes 32800 | tf_op jit(solution)/shard_map/ppermute | solution.py:290
  (138 shorter events, 20.2 us)
Async XLA Ops:
  6.4 1.7 %collective-permute-start.1 = (f32[4,128,128]{2,1,0:T(8,128)S(1)}, f32[4,128,128]{2,1,0:T(8,128)S(1)}, u32[]{:S(2)}, u32[]{:S(2)}) collective-permute-start(f32[4,128,128]{2,1,0:T(8,128)S(1)} %get-tuple-element.44), channel_id=1, source_target_pairs={{0,1},{1,0},{2,3},{3,2},{4,5},{5,4},{6,7},{7,6},{8,9},{9,8},{10,11... | collective-permute-start | bytes 786440 | tf_op jit(solution)/shard_map/ppermute | solution.py:239
  6.9 4.7 %collective-permute-start.6 = (f32[4,128,128]{2,1,0:T(8,128)S(1)}, f32[4,128,128]{2,1,0:T(8,128)S(1)}, u32[]{:S(2)}, u32[]{:S(2)}) collective-permute-start(f32[4,128,128]{2,1,0:T(8,128)S(1)} %get-tuple-element.46), channel_id=1, source_target_pairs={{0,1},{1,0},{2,3},{3,2},{4,5},{5,4},{6,7},{7,6},{8,9},{9,8},{10,11... | collective-permute-start | bytes 786440 | tf_op jit(solution)/shard_map/ppermute | solution.py:239
  7.6 17.9 %copy-start.20 = (f32[4,128,128]{2,1,0:T(8,128)}, f32[4,128,128]{2,1,0:T(8,128)S(1)}, u32[]{:S(2)}) copy-start(f32[4,128,128]{2,1,0:T(8,128)S(1)} %get-tuple-element.57) | copy-start | bytes 786436
  8.1 9.6 %collective-permute-start.2 = (f32[4,128,128]{2,1,0:T(8,128)S(1)}, f32[4,128,128]{2,1,0:T(8,128)S(1)}, u32[]{:S(2)}, u32[]{:S(2)}) collective-permute-start(f32[4,128,128]{2,1,0:T(8,128)S(1)} %add.244), channel_id=1, source_target_pairs={{0,2},{1,3},{2,0},{3,1},{4,6},{5,7},{6,4},{7,5},{8,10},{9,11},{10,... | collective-permute-start | bytes 786440 | tf_op jit(solution)/shard_map/ppermute | solution.py:243
  11.1 8.4 %collective-permute-start = (f32[4,128,128]{2,1,0:T(8,128)S(1)}, f32[4,128,128]{2,1,0:T(8,128)S(1)}, u32[]{:S(2)}, u32[]{:S(2)}) collective-permute-start(f32[4,128,128]{2,1,0:T(8,128)S(1)} %get-tuple-element.42), channel_id=1, source_target_pairs={{0,1},{1,0},{2,3},{3,2},{4,5},{5,4},{6,7},{7,6},{8,9},{9,8},{10,11... | collective-permute-start | bytes 786440 | tf_op jit(solution)/shard_map/ppermute | solution.py:239
  11.1 9.1 %collective-permute-start.10 = (f32[4,128,128]{2,1,0:T(8,128)S(1)}, f32[4,128,128]{2,1,0:T(8,128)S(1)}, u32[]{:S(2)}, u32[]{:S(2)}) collective-permute-start(f32[4,128,128]{2,1,0:T(8,128)S(1)} %get-tuple-element.58), channel_id=1, source_target_pairs={{0,1},{1,0},{2,3},{3,2},{4,5},{5,4},{6,7},{7,6},{8,9},{9,8},{10,11... | collective-permute-start | bytes 786440 | tf_op jit(solution)/shard_map/ppermute | solution.py:239
  17.7 7.8 %collective-permute-start.11 = (f32[4,128,128]{2,1,0:T(8,128)S(1)}, f32[4,128,128]{2,1,0:T(8,128)S(1)}, u32[]{:S(2)}, u32[]{:S(2)}) collective-permute-start(f32[4,128,128]{2,1,0:T(8,128)S(1)} %add.252), channel_id=1, source_target_pairs={{0,2},{1,3},{2,0},{3,1},{4,6},{5,7},{6,4},{7,5},{8,10},{9,11},{10,... | collective-permute-start | bytes 786440 | tf_op jit(solution)/shard_map/ppermute | solution.py:243
  19.5 7.5 %collective-permute-start.3 = (f32[4,128,128]{2,1,0:T(8,128)S(1)}, f32[4,128,128]{2,1,0:T(8,128)S(1)}, u32[]{:S(2)}, u32[]{:S(2)}) collective-permute-start(f32[4,128,128]{2,1,0:T(8,128)S(1)} %add_add_fusion.1), channel_id=1, source_target_pairs={{12,8},{1,5},{14,10},{3,7},{28,24},{17,21},{30,26},{19,23}} | collective-permute-start | bytes 786440 | tf_op jit(solution)/shard_map/ppermute | solution.py:252
  26.3 1.4 %collective-permute-start.12 = (f32[4,128,128]{2,1,0:T(8,128)S(1)}, f32[4,128,128]{2,1,0:T(8,128)S(1)}, u32[]{:S(2)}, u32[]{:S(2)}) collective-permute-start(f32[4,128,128]{2,1,0:T(8,128)S(1)} %add_add_fusion), channel_id=1, source_target_pairs={{12,8},{1,5},{14,10},{3,7},{28,24},{17,21},{30,26},{19,23}} | collective-permute-start | bytes 786440 | tf_op jit(solution)/shard_map/ppermute | solution.py:252
  27.0 1.4 %collective-permute-start.4 = (f32[4,128,128]{2,1,0:T(8,128)S(1)}, f32[4,128,128]{2,1,0:T(8,128)S(1)}, u32[]{:S(2)}, u32[]{:S(2)}) collective-permute-start(f32[4,128,128]{2,1,0:T(8,128)S(1)} %add.246), channel_id=1, source_target_pairs={{8,4},{5,9},{10,6},{7,11},{24,20},{21,25},{26,22},{23,27}} | collective-permute-start | bytes 786440 | tf_op jit(solution)/shard_map/ppermute | solution.py:252
  27.8 2.1 %collective-permute-start.13 = (f32[4,128,128]{2,1,0:T(8,128)S(1)}, f32[4,128,128]{2,1,0:T(8,128)S(1)}, u32[]{:S(2)}, u32[]{:S(2)}) collective-permute-start(f32[4,128,128]{2,1,0:T(8,128)S(1)} %add.257), channel_id=1, source_target_pairs={{8,4},{5,9},{10,6},{7,11},{24,20},{21,25},{26,22},{23,27}} | collective-permute-start | bytes 786440 | tf_op jit(solution)/shard_map/ppermute | solution.py:252
  28.5 13.9 %collective-permute-start.5 = (f32[4,128,128]{2,1,0:T(8,128)S(1)}, f32[4,128,128]{2,1,0:T(8,128)S(1)}, u32[]{:S(2)}, u32[]{:S(2)}) collective-permute-start(f32[4,128,128]{2,1,0:T(8,128)S(1)} %get-tuple-element.72), channel_id=1, source_target_pairs={{4,0},{9,13},{6,2},{11,15},{20,16},{25,29},{22,18},{27,31}} | collective-permute-start | bytes 786440 | tf_op jit(solution)/shard_map/ppermute | solution.py:252
  29.9 12.6 %copy-start.39 = (f32[4,128,128]{2,1,0:T(8,128)S(1)}, f32[4,128,128]{2,1,0:T(8,128)}, u32[]{:S(2)}) copy-start(f32[4,128,128]{2,1,0:T(8,128)} %copy-done.38) | copy-start | bytes 786436
  29.9 19.0 %collective-permute-start.14 = (f32[4,128,128]{2,1,0:T(8,128)S(1)}, f32[4,128,128]{2,1,0:T(8,128)S(1)}, u32[]{:S(2)}, u32[]{:S(2)}) collective-permute-start(f32[4,128,128]{2,1,0:T(8,128)S(1)} %get-tuple-element.70), channel_id=1, source_target_pairs={{4,0},{9,13},{6,2},{11,15},{20,16},{25,29},{22,18},{27,31}} | collective-permute-start | bytes 786440 | tf_op jit(solution)/shard_map/ppermute | solution.py:252
  43.3 8.1 %collective-permute-start.7 = (f32[4,128,128]{2,1,0:T(8,128)S(1)}, f32[4,128,128]{2,1,0:T(8,128)}, u32[]{:S(2)}, u32[]{:S(2)}) collective-permute-start(f32[4,128,128]{2,1,0:T(8,128)S(1)} %get-tuple-element.76), channel_id=1, source_target_pairs={{0,2},{1,3},{2,0},{3,1},{4,6},{5,7},{6,4},{7,5},{8,10},{9,11},{10,... | collective-permute-start | bytes 786440 | tf_op jit(solution)/shard_map/ppermute | solution.py:243
  49.8 13.1 %collective-permute-start.15 = (f32[4,128,128]{2,1,0:T(8,128)}, f32[4,128,128]{2,1,0:T(8,128)}, u32[]{:S(2)}, u32[]{:S(2)}) collective-permute-start(f32[4,128,128]{2,1,0:T(8,128)} %get-tuple-element.74), channel_id=1, source_target_pairs={{0,2},{1,3},{2,0},{3,1},{4,6},{5,7},{6,4},{7,5},{8,10},{9,11},{10,... | collective-permute-start | bytes 786440 | tf_op jit(solution)/shard_map/ppermute | solution.py:243
  51.3 11.9 %collective-permute-start.8 = (f32[4,128,128]{2,1,0:T(8,128)}, f32[4,128,128]{2,1,0:T(8,128)}, u32[]{:S(2)}, u32[]{:S(2)}) collective-permute-start(f32[4,128,128]{2,1,0:T(8,128)} %get-tuple-element.77.refs_8_), channel_id=1, source_target_pairs={{0,1},{1,0},{2,3},{3,2},{4,5},{5,4},{6,7},{7,6},{8,9},{9,8},{10,11... | collective-permute-start | bytes 786440 | tf_op jit(solution)/shard_map/ppermute | solution.py:239
  51.4 11.9 %collective-permute-start.9 = (f32[4,128,128]{2,1,0:T(8,128)}, f32[4,128,128]{2,1,0:T(8,128)}, u32[]{:S(2)}, u32[]{:S(2)}) collective-permute-start(f32[4,128,128]{2,1,0:T(8,128)} %collective-permute-done.7.refs_9_), channel_id=1, source_target_pairs={{0,1},{1,0},{2,3},{3,2},{4,5},{5,4},{6,7},{7,6},{8,9},{9,8},{10,11... | collective-permute-start | bytes 786440 | tf_op jit(solution)/shard_map/ppermute | solution.py:239
  59.8 15.7 %collective-permute-start.16 = (f32[4,128,128]{2,1,0:T(8,128)}, f32[4,128,128]{2,1,0:T(8,128)}, u32[]{:S(2)}, u32[]{:S(2)}) collective-permute-start(f32[4,128,128]{2,1,0:T(8,128)} %get-tuple-element.75.refs_8_), channel_id=1, source_target_pairs={{0,1},{1,0},{2,3},{3,2},{4,5},{5,4},{6,7},{7,6},{8,9},{9,8},{10,11... | collective-permute-start | bytes 786440 | tf_op jit(solution)/shard_map/ppermute | solution.py:239
  62.9 12.6 %collective-permute-start.17 = (f32[4,128,128]{2,1,0:T(8,128)}, f32[4,128,128]{2,1,0:T(8,128)}, u32[]{:S(2)}, u32[]{:S(2)}) collective-permute-start(f32[4,128,128]{2,1,0:T(8,128)} %collective-permute-done.15.refs_9_), channel_id=1, source_target_pairs={{0,1},{1,0},{2,3},{3,2},{4,5},{5,4},{6,7},{7,6},{8,9},{9,8},{10,11... | collective-permute-start | bytes 786440 | tf_op jit(solution)/shard_map/ppermute | solution.py:239
  67.7 11.8 %collective-permute-start.18 = (f32[8,64,128]{2,1,0:T(8,128)}, f32[8,64,128]{2,1,0:T(8,128)}, u32[]{:S(2)}, u32[]{:S(2)}) collective-permute-start(f32[8,64,128]{2,1,0:T(8,128)} %dynamic-slice_bitcast_fusion.1), channel_id=1, source_target_pairs={{0,1},{1,0},{2,3},{3,2},{4,5},{5,4},{6,7},{7,6},{8,9},{9,8},{10,11... | collective-permute-start | bytes 786440 | tf_op jit(solution)/shard_map/ppermute | solution.py:239
  79.2 5.0 %collective-permute-start.22 = (f32[8,64,128]{2,1,0:T(8,128)S(1)}, f32[8,64,128]{2,1,0:T(8,128)S(1)}, u32[]{:S(2)}, u32[]{:S(2)}) collective-permute-start(f32[8,64,128]{2,1,0:T(8,128)S(1)} %dynamic-slice_bitcast_fusion), channel_id=1, source_target_pairs={{0,1},{1,0},{2,3},{3,2},{4,5},{5,4},{6,7},{7,6},{8,9},{9,8},{10,11... | collective-permute-start | bytes 786440 | tf_op jit(solution)/shard_map/ppermute | solution.py:239
  80.6 5.7 %collective-permute-start.21 = (f32[2,64,128]{2,1,0:T(8,128)S(1)}, f32[2,64,128]{2,1,0:T(8,128)S(1)}, u32[]{:S(2)}, u32[]{:S(2)}) collective-permute-start(f32[2,64,128]{2,1,0:T(8,128)S(1)} %get-tuple-element.82), channel_id=1, source_target_pairs={{0,18},{1,19},{2,16},{3,17},{4,22},{5,23},{6,20},{7,21},{8,26},{9,... | collective-permute-start | bytes 196616 | tf_op jit(solution)/shard_map/ppermute | solution.py:280
  82.1 5.7 %collective-permute-start.20 = (f32[2,64,128]{2,1,0:T(8,128)S(1)}, f32[2,64,128]{2,1,0:T(8,128)S(1)}, u32[]{:S(2)}, u32[]{:S(2)}) collective-permute-start(f32[2,64,128]{2,1,0:T(8,128)S(1)} %get-tuple-element.83), channel_id=1, source_target_pairs={{0,16},{1,17},{2,18},{3,19},{4,20},{5,21},{6,22},{7,23},{8,24},{9,... | collective-permute-start | bytes 196616 | tf_op jit(solution)/shard_map/ppermute | solution.py:280
  82.7 5.2 %collective-permute-start.19 = (f32[2,64,128]{2,1,0:T(8,128)S(1)}, f32[2,64,128]{2,1,0:T(8,128)S(1)}, u32[]{:S(2)}, u32[]{:S(2)}) collective-permute-start(f32[2,64,128]{2,1,0:T(8,128)S(1)} %get-tuple-element.81), channel_id=1, source_target_pairs={{0,2},{1,3},{2,0},{3,1},{4,6},{5,7},{6,4},{7,5},{8,10},{9,11},{10,... | collective-permute-start | bytes 196616 | tf_op jit(solution)/shard_map/ppermute | solution.py:280
  84.2 10.7 %copy-start.37 = (bf16[8,128,128]{2,1,0:T(8,128)(2,1)S(1)}, bf16[8,128,128]{2,1,0:T(8,128)(2,1)}, u32[]{:S(2)}) copy-start(bf16[8,128,128]{2,1,0:T(8,128)(2,1)} %copy-done.36) | copy-start | bytes 786436
  84.3 5.6 %collective-permute-start.25 = (f32[2,64,128]{2,1,0:T(8,128)S(1)}, f32[2,64,128]{2,1,0:T(8,128)S(1)}, u32[]{:S(2)}, u32[]{:S(2)}) collective-permute-start(f32[2,64,128]{2,1,0:T(8,128)S(1)} %get-tuple-element.79), channel_id=1, source_target_pairs={{0,18},{1,19},{2,16},{3,17},{4,22},{5,23},{6,20},{7,21},{8,26},{9,... | collective-permute-start | bytes 196616 | tf_op jit(solution)/shard_map/ppermute | solution.py:280
  85.8 4.3 %collective-permute-start.24 = (f32[2,64,128]{2,1,0:T(8,128)S(1)}, f32[2,64,128]{2,1,0:T(8,128)S(1)}, u32[]{:S(2)}, u32[]{:S(2)}) collective-permute-start(f32[2,64,128]{2,1,0:T(8,128)S(1)} %get-tuple-element.80), channel_id=1, source_target_pairs={{0,16},{1,17},{2,18},{3,19},{4,20},{5,21},{6,22},{7,23},{8,24},{9,... | collective-permute-start | bytes 196616 | tf_op jit(solution)/shard_map/ppermute | solution.py:280
  86.3 4.3 %collective-permute-start.23 = (f32[2,64,128]{2,1,0:T(8,128)S(1)}, f32[2,64,128]{2,1,0:T(8,128)S(1)}, u32[]{:S(2)}, u32[]{:S(2)}) collective-permute-start(f32[2,64,128]{2,1,0:T(8,128)S(1)} %get-tuple-element.78), channel_id=1, source_target_pairs={{0,2},{1,3},{2,0},{3,1},{4,6},{5,7},{6,4},{7,5},{8,10},{9,11},{10,... | collective-permute-start | bytes 196616 | tf_op jit(solution)/shard_map/ppermute | solution.py:280
  90.7 6.4 %collective-permute-start.28 = (f32[64,128]{1,0:T(8,128)S(1)}, f32[64,128]{1,0:T(8,128)S(1)}, u32[]{:S(2)}, u32[]{:S(2)}) collective-permute-start(f32[64,128]{1,0:T(8,128)S(1)} %get-tuple-element.86), channel_id=1, source_target_pairs={{0,12},{1,13},{2,14},{3,15},{4,0},{5,1},{6,2},{7,3},{8,4},{9,5},{1... | collective-permute-start | bytes 98312 | tf_op jit(solution)/shard_map/ppermute | solution.py:290
  90.7 6.3 %collective-permute-start.27 = (f32[64,128]{1,0:T(8,128)S(1)}, f32[64,128]{1,0:T(8,128)S(1)}, u32[]{:S(2)}, u32[]{:S(2)}) collective-permute-start(f32[64,128]{1,0:T(8,128)S(1)} %get-tuple-element.85), channel_id=1, source_target_pairs={{0,8},{1,9},{2,10},{3,11},{4,12},{5,13},{6,14},{7,15},{8,0},{9,1},... | collective-permute-start | bytes 98312 | tf_op jit(solution)/shard_map/ppermute | solution.py:290
  93.6 5.7 %collective-permute-start.26 = (f32[64,128]{1,0:T(8,128)S(1)}, f32[64,128]{1,0:T(8,128)S(1)}, u32[]{:S(2)}, u32[]{:S(2)}) collective-permute-start(f32[64,128]{1,0:T(8,128)S(1)} %get-tuple-element.84), channel_id=1, source_target_pairs={{0,4},{1,5},{2,6},{3,7},{4,8},{5,9},{6,10},{7,11},{8,12},{9,13},{1... | collective-permute-start | bytes 98312 | tf_op jit(solution)/shard_map/ppermute | solution.py:290
  (39 other events, 129.3 us)
